TPU v7x, 32 devices: a whole 2x2x4 slice. The times are simulated.
32 devices in a mesh: seq: 8 (over y, x, core), head: 4 (over z).
Axes of the slice: x: 2, y: 2, z: 4, core: 2. Of those that a mesh axis runs over, the one named last changes fastest.
Arguments:
- queries: bfloat16 [6144, 2048], P(('seq', 'head')), may hold values from -8 to 8
- keys: bfloat16 [6144, 2048], P(('seq', 'head')), may hold values from -8 to 8
- values: bfloat16 [6144, 2048], P(('seq', 'head')), may hold values from -6 to 6
- cotangent: bfloat16 [6144, 2048], P(('seq', 'head')), may hold values from -6 to 6
- neighbours: int32 [96, 27], replicated, may hold values from -1 to 95, as said below
Outputs:
- output: bfloat16 [6144, 2048], P(('seq', 'head'))
- grad_query: bfloat16 [6144, 2048], P(('seq', 'head'))
- grad_key: bfloat16 [6144, 2048], P(('seq', 'head'))
- grad_value: bfloat16 [6144, 2048], P(('seq', 'head'))
Inputs may be any that keep to these rules, and one draw needn't show every extreme that they name: `neighbours`: row g lists distinct tiles, always g itself; a listed tile's frame, tile row and tile column each differ from g's by at most one; -1 marks an empty slot; slots stand in any order.
All inputs are finite; a program needn't handle non-finite values.
Results may differ from a plain program's by a relative error of at most 0.015.
Values may be sent and summed in bfloat16 or wider, within the bound.
A program may use at most 128 MiB of HBM per device.

v0:
```python
import math

import jax
import jax.numpy as jnp
from jax import lax
from jax.sharding import PartitionSpec as P

TILE = 64
TILES_F = 12
SLOTS = 27
HD = 128
F_DEV = 1


masked_score = -1e30


def extended(cells, sides, width):
    for axis, dim in sides:
        count = lax.axis_size(axis)
        ends = count - 1
        head = lax.slice_in_dim(cells, 0, width, axis=dim)
        tail = lax.slice_in_dim(cells, cells.shape[dim] - width, cells.shape[dim], axis=dim)
        cells = jnp.concatenate(
            [
                lax.ppermute(tail, axis, [(i, (i + 1) % count) for i in range(ends)]),
                cells,
                lax.ppermute(head, axis, [((i + 1) % count, i) for i in range(ends)]),
            ],
            axis=dim,
        )
    return cells


def shifted(array, axis, by):
    peers = lax.axis_size(axis)
    pairs = [(i, i + by) for i in range(peers) if 0 <= i + by < peers]
    return lax.ppermute(array, axis, pairs)


def split_heads(rows, head_count):
    return rows.reshape(rows.shape[0], rows.shape[1], head_count, rows.shape[2] // head_count)


def tile_probs(query_heads, key_heads, key_mask, log_total, score_scale):
    scores = (
        jnp.einsum("btnd,bknd->bntk", query_heads, key_heads, preferred_element_type=jnp.float32)
        * score_scale
    )
    scores = jnp.where(key_mask[:, None, None, :], scores, masked_score)
    row_max = jnp.max(scores, axis=-1, keepdims=True)
    log_total = row_max + jnp.log(jnp.sum(jnp.exp(scores - row_max), axis=-1, keepdims=True))
    return (jnp.exp(scores - log_total), log_total)


def pair_grads(probs, probs_low, grad_dot, query_heads, value_heads, cot_heads, score_scale):
    grad_prob = jnp.einsum(
        "btnd,bknd->bntk", cot_heads, value_heads, preferred_element_type=jnp.float32
    )
    grad_score = (
        probs * (grad_prob - jnp.transpose(grad_dot, (0, 2, 1))[..., None]) * score_scale
    ).astype(jnp.bfloat16)
    grad_key = jnp.einsum(
        "bntk,btnd->bknd", grad_score, query_heads, preferred_element_type=jnp.float32
    )
    grad_value = jnp.einsum(
        "bntk,btnd->bknd", probs_low, cot_heads, preferred_element_type=jnp.float32
    )
    block_tiles, key_len = (grad_key.shape[0], grad_key.shape[1])
    grad_pair = jnp.concatenate(
        [grad_key.reshape(block_tiles, key_len, -1), grad_value.reshape(block_tiles, key_len, -1)],
        axis=-1,
    )
    return (grad_score, grad_pair)


def attend_both(query_blk, kv_near, key_mask, cot_blk, head_count):
    feature_width = query_blk.shape[2]
    score_scale = 1.0 / math.sqrt(feature_width // head_count)
    query_heads = split_heads(query_blk, head_count)
    key_heads = split_heads(kv_near[:, :, :feature_width], head_count)
    value_heads = split_heads(kv_near[:, :, feature_width:], head_count)
    cot_heads = split_heads(cot_blk, head_count)
    probs, log_total = tile_probs(query_heads, key_heads, key_mask, None, score_scale)
    probs_low = probs.astype(jnp.bfloat16)
    output = jnp.einsum(
        "bntk,bknd->btnd", probs_low, value_heads, preferred_element_type=jnp.float32
    ).astype(jnp.bfloat16)
    grad_dot = jnp.sum(cot_heads.astype(jnp.float32) * output.astype(jnp.float32), axis=-1)
    grad_score, grad_pair = pair_grads(
        probs, probs_low, grad_dot, query_heads, value_heads, cot_heads, score_scale
    )
    grad_query = jnp.einsum(
        "bntk,bknd->btnd", grad_score, key_heads, preferred_element_type=jnp.float32
    ).astype(jnp.bfloat16)
    shape_rows = query_blk.shape
    stats = jnp.concatenate([jnp.transpose(log_total[..., 0], (0, 2, 1)), grad_dot], axis=-1)
    return (output.reshape(shape_rows), grad_query.reshape(shape_rows), stats, grad_pair)


def shards(queries, keys, values, cotangent, neighbours):
    query_seq = lax.all_to_all(queries, "head", split_axis=1, concat_axis=0, tiled=True)
    keys_seq, values_seq = (
        lax.all_to_all(keys, "head", split_axis=1, concat_axis=0, tiled=True),
        lax.all_to_all(values, "head", split_axis=1, concat_axis=0, tiled=True),
    )
    cot_seq = lax.all_to_all(cotangent, "head", split_axis=1, concat_axis=0, tiled=True)
    feature_width = query_seq.shape[1]
    head_count = feature_width // HD
    frame_tok = TILE * TILES_F
    own_tiles = F_DEV * TILES_F
    ext_tiles = own_tiles + 2 * TILES_F
    all_tiles = lax.axis_size("seq") * own_tiles
    first_tile = lax.axis_index("seq") * own_tiles
    base_tile = first_tile - TILES_F
    block_tiles = TILES_F // 4
    kv_pair = jnp.concatenate([keys_seq, values_seq], axis=1)
    kv_ext = extended(kv_pair, (("seq", 0),), frame_tok)
    pair_tiles = jnp.concatenate(
        [
            kv_ext.reshape(ext_tiles, TILE, 2 * feature_width),
            jnp.zeros((1, TILE, 2 * feature_width), jnp.bfloat16),
        ],
        axis=0,
    )

    def near_pairs(index_blk):
        return jnp.take(pair_tiles, index_blk, axis=0).reshape(
            index_blk.shape[0], SLOTS * TILE, 2 * feature_width
        )

    query_tiles = query_seq.reshape(own_tiles, TILE, feature_width)
    cot_tiles = cot_seq.reshape(own_tiles, TILE, feature_width)
    tile_ids = first_tile + jnp.arange(own_tiles, dtype=jnp.int32)
    present = (tile_ids >= 0) & (tile_ids < all_tiles)
    rows_listed = jnp.take(neighbours, jnp.clip(tile_ids, 0, neighbours.shape[0] - 1), axis=0)
    relative = rows_listed - base_tile
    usable = present[:, None] & (rows_listed >= 0) & (relative >= 0) & (relative < ext_tiles)
    own_index = jnp.where(usable, relative, ext_tiles)

    def own_step(grad_buffer, block_id):
        first_row = block_id * block_tiles
        query_blk = lax.dynamic_slice_in_dim(query_tiles, first_row, block_tiles, 0)
        cot_blk = lax.dynamic_slice_in_dim(cot_tiles, first_row, block_tiles, 0)
        index_blk = lax.dynamic_slice_in_dim(own_index, first_row, block_tiles, 0)
        usable_blk = lax.dynamic_slice_in_dim(usable, first_row, block_tiles, 0)
        key_mask = jnp.repeat(usable_blk, TILE, axis=1)
        output, grad_query, stats, grad_pair = attend_both(
            query_blk, near_pairs(index_blk), key_mask, cot_blk, head_count
        )
        grad_buffer = grad_buffer.at[index_blk].add(
            grad_pair.reshape(block_tiles, SLOTS, TILE, 2 * feature_width)
        )
        return (grad_buffer, (output, grad_query, stats))

    start_buffer = jnp.zeros((ext_tiles + 1, TILE, 2 * feature_width), jnp.float32)
    grad_buffer, (outputs, grad_queries, own_stats) = lax.scan(
        own_step, start_buffer, jnp.arange(own_tiles // block_tiles, dtype=jnp.int32)
    )
    own_rows = F_DEV * frame_tok
    output_rows = outputs.reshape(own_rows, feature_width)
    grad_query_rows = grad_queries.reshape(own_rows, feature_width)
    upper_part = grad_buffer[:TILES_F]
    lower_part = grad_buffer[TILES_F + own_tiles : ext_tiles]
    from_next = shifted(upper_part.astype(jnp.bfloat16), "seq", -1).astype(upper_part.dtype)
    from_prev = shifted(lower_part.astype(jnp.bfloat16), "seq", 1).astype(lower_part.dtype)
    own_grad = grad_buffer[TILES_F : TILES_F + own_tiles]
    own_grad = own_grad.at[:TILES_F].add(from_prev)
    own_grad = own_grad.at[own_tiles - TILES_F :].add(from_next)
    grad_rows = own_grad.reshape(own_rows, 2 * feature_width)
    grad_key_rows = grad_rows[:, :feature_width].astype(jnp.bfloat16)
    grad_value_rows = grad_rows[:, feature_width:].astype(jnp.bfloat16)
    output, grad_query, grad_key, grad_value = (
        lax.all_to_all(output_rows, "head", split_axis=0, concat_axis=1, tiled=True),
        lax.all_to_all(grad_query_rows, "head", split_axis=0, concat_axis=1, tiled=True),
        lax.all_to_all(grad_key_rows, "head", split_axis=0, concat_axis=1, tiled=True),
        lax.all_to_all(grad_value_rows, "head", split_axis=0, concat_axis=1, tiled=True),
    )
    return (output, grad_query, grad_key, grad_value)


def solution(mesh):
    placed = (
        P(("seq", "head"), None),
        P(("seq", "head"), None),
        P(("seq", "head"), None),
        P(("seq", "head"), None),
        P(),
    )
    return jax.shard_map(
        shards,
        mesh=mesh,
        in_specs=placed,
        out_specs=(
            P(("seq", "head"), None),
            P(("seq", "head"), None),
            P(("seq", "head"), None),
            P(("seq", "head"), None),
        ),
        check_vma=False,
    )
```

profile of v0, /device:TPU:2, one launch (start us, length us, event | category | flops | bytes accessed | tf_op | source)
XLA Modules:
  0.0 944.0 jit_solution(10186335645468660926)
XLA Ops:
  9.9 18.0 %all-to-all-done.1 = bf16[192,4,512]{2,0,1:T(8,128)(2,1)S(1)} async-done(((bf16[192,4,512]{2,0,1:T(8,128)(2,1)}), bf16[192,4,512]{2,0,1:T(8,128)(2,1)S(1)}, u32[]{:S(2)}, u32[]{:S(2)}) %all-to-all-start.1) | async-done | bytes 786464 | tf_op jit(solution)/shard_map/all_to_all | solution.py:104
  32.5 18.6 %all-to-all-done.2 = bf16[192,4,512]{2,0,1:T(8,128)(2,1)S(1)} async-done(((bf16[192,4,512]{2,0,1:T(8,128)(2,1)}), bf16[192,4,512]{2,0,1:T(8,128)(2,1)S(1)}, u32[]{:S(2)}, u32[]{:S(2)}) %all-to-all-start.2) | async-done | bytes 786464 | tf_op jit(solution)/shard_map/all_to_all | solution.py:105
  102.2 734.4 %while.18 = (s32[]{:T(128)}, f32[37,64,1024]{2,1,0:T(8,128)}, bf16[4,3,64,512]{3,2,1,0:T(8,128)(2,1)}, bf16[4,3,64,512]{3,2,1,0:T(8,128)(2,1)}, s32[4]{0:T(128)S...) while((s32[]{:T(128)}, f32[37,64,1024]{2,1,0:T(8,128)}, ...), condition=%wide.region_5.6_spmd, body=%wide.region_0.5_spmd.sunk | while | flops 2073526272 | bytes 424471488 | solution.py:157
  113.4 14.2 %copy.158 = bf16[3,1728,1024]{1,2,0:T(8,128)(2,1)} copy(bf16[3,1728,1024]{2,1,0:T(8,128)(2,1)} %bitcast.136) | data formatting | bytes 21233664 | tf_op jit(solution)/shard_map/while/body/eval_jaxpr/jit(_take)/gather | solution.py:128
  166.6 13.3 %copy.159 = f32[3,1728,4,128]{3,2,1,0:T(4,128)} copy(f32[3,1728,4,128]{3,1,2,0:T(8,128)S(1)} %convolution_bitcast_fusion.4) | data formatting | bytes 21233664 | tf_op jit(solution)/shard_map/while/body/eval_jaxpr/bntk,btnd->bknd/transpose | solution.py:66
  194.7 13.3 %copy.160 = f32[3,1728,4,128]{3,2,1,0:T(4,128)} copy(f32[3,1728,4,128]{3,1,2,0:T(8,128)S(1)} %convolution_bitcast_fusion.5) | data formatting | bytes 21233664 | tf_op jit(solution)/shard_map/while/body/eval_jaxpr/bntk,btnd->bknd/transpose | solution.py:63
  221.1 15.6 %pad_maximum_fusion.4 = f32[3,27,64,1024]{3,2,1,0:T(8,128)} fusion(f32[3,27,64,512]{3,2,1,0:T(8,128)} %concatenate.26, f32[3,27,64,512]{3,2,1,0:T(8,128)} %concatenate.27), kind=kLoop, calls=%fused_computation.3.clone.1 | loop fusion | flops 5308416 | bytes 42467328 | tf_op jit(solution)/shard_map/while/body/eval_jaxpr/concatenate | solution.py:70
  236.8 49.3 %scatter_fusion = f32[37,64,1024]{2,1,0:T(8,128)} fusion(f32[37,64,1024]{2,1,0:T(8,128)} %get-tuple-element.236, s32[81]{0:T(128)S(1)} %reshape.231, f32[81,64,1024]{2,1,0:T(8,128)} %bitcast.127), kind=kCustom, calls=%fused_computation.2.clone.1 | custom fusion | flops 5308416 | bytes 63701316 | tf_op jit(solution)/shard_map/while/body/eval_jaxpr/scatter-add | solution.py:151
  297.3 14.2 %copy.158 = bf16[3,1728,1024]{1,2,0:T(8,128)(2,1)} copy(bf16[3,1728,1024]{2,1,0:T(8,128)(2,1)} %bitcast.136) | data formatting | bytes 21233664 | tf_op jit(solution)/shard_map/while/body/eval_jaxpr/jit(_take)/gather | solution.py:128
  350.5 13.3 %copy.159 = f32[3,1728,4,128]{3,2,1,0:T(4,128)} copy(f32[3,1728,4,128]{3,1,2,0:T(8,128)S(1)} %convolution_bitcast_fusion.4) | data formatting | bytes 21233664 | tf_op jit(solution)/shard_map/while/body/eval_jaxpr/bntk,btnd->bknd/transpose | solution.py:66
  378.6 13.3 %copy.160 = f32[3,1728,4,128]{3,2,1,0:T(4,128)} copy(f32[3,1728,4,128]{3,1,2,0:T(8,128)S(1)} %convolution_bitcast_fusion.5) | data formatting | bytes 21233664 | tf_op jit(solution)/shard_map/while/body/eval_jaxpr/bntk,btnd->bknd/transpose | solution.py:63
  405.0 15.6 %pad_maximum_fusion.4 = f32[3,27,64,1024]{3,2,1,0:T(8,128)} fusion(f32[3,27,64,512]{3,2,1,0:T(8,128)} %concatenate.26, f32[3,27,64,512]{3,2,1,0:T(8,128)} %concatenate.27), kind=kLoop, calls=%fused_computation.3.clone.1 | loop fusion | flops 5308416 | bytes 42467328 | tf_op jit(solution)/shard_map/while/body/eval_jaxpr/concatenate | solution.py:70
  420.6 48.7 %scatter_fusion = f32[37,64,1024]{2,1,0:T(8,128)} fusion(f32[37,64,1024]{2,1,0:T(8,128)} %get-tuple-element.236, s32[81]{0:T(128)S(1)} %reshape.231, f32[81,64,1024]{2,1,0:T(8,128)} %bitcast.127), kind=kCustom, calls=%fused_computation.2.clone.1 | custom fusion | flops 5308416 | bytes 63701316 | tf_op jit(solution)/shard_map/while/body/eval_jaxpr/scatter-add | solution.py:151
  480.6 14.2 %copy.158 = bf16[3,1728,1024]{1,2,0:T(8,128)(2,1)} copy(bf16[3,1728,1024]{2,1,0:T(8,128)(2,1)} %bitcast.136) | data formatting | bytes 21233664 | tf_op jit(solution)/shard_map/while/body/eval_jaxpr/jit(_take)/gather | solution.py:128
  533.8 13.3 %copy.159 = f32[3,1728,4,128]{3,2,1,0:T(4,128)} copy(f32[3,1728,4,128]{3,1,2,0:T(8,128)S(1)} %convolution_bitcast_fusion.4) | data formatting | bytes 21233664 | tf_op jit(solution)/shard_map/while/body/eval_jaxpr/bntk,btnd->bknd/transpose | solution.py:66
  561.9 13.3 %copy.160 = f32[3,1728,4,128]{3,2,1,0:T(4,128)} copy(f32[3,1728,4,128]{3,1,2,0:T(8,128)S(1)} %convolution_bitcast_fusion.5) | data formatting | bytes 21233664 | tf_op jit(solution)/shard_map/while/body/eval_jaxpr/bntk,btnd->bknd/transpose | solution.py:63
  588.3 15.6 %pad_maximum_fusion.4 = f32[3,27,64,1024]{3,2,1,0:T(8,128)} fusion(f32[3,27,64,512]{3,2,1,0:T(8,128)} %concatenate.26, f32[3,27,64,512]{3,2,1,0:T(8,128)} %concatenate.27), kind=kLoop, calls=%fused_computation.3.clone.1 | loop fusion | flops 5308416 | bytes 42467328 | tf_op jit(solution)/shard_map/while/body/eval_jaxpr/concatenate | solution.py:70
  603.9 49.0 %scatter_fusion = f32[37,64,1024]{2,1,0:T(8,128)} fusion(f32[37,64,1024]{2,1,0:T(8,128)} %get-tuple-element.236, s32[81]{0:T(128)S(1)} %reshape.231, f32[81,64,1024]{2,1,0:T(8,128)} %bitcast.127), kind=kCustom, calls=%fused_computation.2.clone.1 | custom fusion | flops 5308416 | bytes 63701316 | tf_op jit(solution)/shard_map/while/body/eval_jaxpr/scatter-add | solution.py:151
  664.2 14.2 %copy.158 = bf16[3,1728,1024]{1,2,0:T(8,128)(2,1)} copy(bf16[3,1728,1024]{2,1,0:T(8,128)(2,1)} %bitcast.136) | data formatting | bytes 21233664 | tf_op jit(solution)/shard_map/while/body/eval_jaxpr/jit(_take)/gather | solution.py:128
  771.9 15.6 %pad_maximum_fusion.4 = f32[3,27,64,1024]{3,2,1,0:T(8,128)} fusion(f32[3,27,64,512]{3,2,1,0:T(8,128)} %concatenate.26, f32[3,27,64,512]{3,2,1,0:T(8,128)} %concatenate.27), kind=kLoop, calls=%fused_computation.3.clone.1 | loop fusion | flops 5308416 | bytes 42467328 | tf_op jit(solution)/shard_map/while/body/eval_jaxpr/concatenate | solution.py:70
  787.5 48.9 %scatter_fusion = f32[37,64,1024]{2,1,0:T(8,128)} fusion(f32[37,64,1024]{2,1,0:T(8,128)} %get-tuple-element.236, s32[81]{0:T(128)S(1)} %reshape.231, f32[81,64,1024]{2,1,0:T(8,128)} %bitcast.127), kind=kCustom, calls=%fused_computation.2.clone.1 | custom fusion | flops 5308416 | bytes 63701316 | tf_op jit(solution)/shard_map/while/body/eval_jaxpr/scatter-add | solution.py:151
  868.4 20.5 %collective-permute-done.3 = bf16[12,64,1024]{2,1,0:T(8,128)(2,1)} collective-permute-done((bf16[12,64,1024]{2,1,0:T(8,128)(2,1)S(1)}, bf16[12,64,1024]{2,1,0:T(8,128)(2,1)}, u32[]{:S(2)}, u32[]{:S(2)}) %collective-permute-start.3) | collective-permute-done | bytes 1572896 | tf_op jit(solution)/shard_map/ppermute | solution.py:38
  893.6 25.9 %all_to_all.146 = bf16[4,192,512]{2,1,0:T(8,128)(2,1)S(1)} all-to-all(bf16[4,192,512]{2,1,0:T(8,128)(2,1)S(1)} %bitcast.151), channel_id=1, replica_groups=mesh['seq'=8,'head'=4] {'head'}, dimensions={0} | all-to-all | bytes 1572864 | tf_op jit(solution)/shard_map/all_to_all | solution.py:176
  926.0 17.0 %all-to-all-done.7 = bf16[4,192,512]{2,1,0:T(8,128)(2,1)S(1)} async-done(((bf16[4,192,512]{2,1,0:T(8,128)(2,1)}), bf16[4,192,512]{2,1,0:T(8,128)(2,1)S(1)}, u32[]{:S(2)}, u32[]{:S(2)}) %all-to-all-start.7) | async-done | bytes 786464 | tf_op jit(solution)/shard_map/all_to_all | solution.py:177
  (276 shorter events, 445.1 us)
Async XLA Ops:
  2.8 57.6 %copy-start.6 = (bf16[192,2048]{1,0:T(8,128)(2,1)S(1)}, bf16[192,2048]{1,0:T(8,128)(2,1)}, u32[]{:S(2)}) copy-start(bf16[192,2048]{1,0:T(8,128)(2,1)} %param.18) | copy-start | bytes 2359300
  2.8 25.1 %all-to-all-start.1 = ((bf16[192,4,512]{2,0,1:T(8,128)(2,1)}), bf16[192,4,512]{2,0,1:T(8,128)(2,1)S(1)}, u32[]{:S(2)}, u32[]{:S(2)}) async-start(bf16[192,4,512]{2,0,1:T(8,128)(2,1)} %bitcast.83), calls=%async_computation.1 | async-start | bytes 1572864 | tf_op jit(solution)/shard_map/all_to_all | solution.py:104
  27.9 49.8 %copy-start.9 = (s32[96,27]{0,1:T(8,128)S(1)}, s32[96,27]{0,1:T(8,128)}, u32[]{:S(2)}) copy-start(s32[96,27]{0,1:T(8,128)} %param.19) | copy-start | bytes 31108
  27.9 23.2 %all-to-all-start.2 = ((bf16[192,4,512]{2,0,1:T(8,128)(2,1)}), bf16[192,4,512]{2,0,1:T(8,128)(2,1)S(1)}, u32[]{:S(2)}, u32[]{:S(2)}) async-start(bf16[192,4,512]{2,0,1:T(8,128)(2,1)} %bitcast.82), calls=%async_computation.2 | async-start | bytes 1572864 | tf_op jit(solution)/shard_map/all_to_all | solution.py:105
  51.1 23.1 %all-to-all-start = ((bf16[192,4,512]{2,0,1:T(8,128)(2,1)}), bf16[192,4,512]{2,0,1:T(8,128)(2,1)S(1)}, u32[]{:S(2)}, u32[]{:S(2)}) async-start(bf16[192,4,512]{2,0,1:T(8,128)(2,1)} %bitcast.84), calls=%async_computation | async-start | bytes 1572864 | tf_op jit(solution)/shard_map/all_to_all | solution.py:102
  56.0 34.0 %collective-permute-start.1 = (bf16[768,1024]{1,0:T(8,128)(2,1)}, bf16[768,1024]{1,0:T(8,128)(2,1)}, u32[]{:S(2)}, u32[]{:S(2)}) collective-permute-start(bf16[768,1024]{1,0:T(8,128)(2,1)} %pad_maximum_fusion.2), channel_id=1, source_target_pairs={{4,0},{8,4},{12,8},{16,12},{20,16},{24,20},{28,24},{5,1},{9,5},{13... | collective-permute-start | bytes 4718600 | tf_op jit(solution)/shard_map/ppermute | solution.py:28
  58.0 32.1 %collective-permute-start = (bf16[768,1024]{1,0:T(8,128)(2,1)}, bf16[768,1024]{1,0:T(8,128)(2,1)}, u32[]{:S(2)}, u32[]{:S(2)}) collective-permute-start(bf16[768,1024]{1,0:T(8,128)(2,1)} %pad_maximum_fusion.2), channel_id=1, source_target_pairs={{0,4},{4,8},{8,12},{12,16},{16,20},{20,24},{24,28},{1,5},{5,9},{9,... | collective-permute-start | bytes 4718600 | tf_op jit(solution)/shard_map/ppermute | solution.py:26
  74.2 23.1 %all-to-all-start.3 = ((bf16[192,4,512]{2,0,1:T(8,128)(2,1)}), bf16[192,4,512]{2,0,1:T(8,128)(2,1)S(1)}, u32[]{:S(2)}, u32[]{:S(2)}) async-start(bf16[192,4,512]{2,0,1:T(8,128)(2,1)} %bitcast.146), calls=%async_computation.3 | async-start | bytes 1572864 | tf_op jit(solution)/shard_map/all_to_all | solution.py:107
  236.7 49.3 %copy-start.2 = (bf16[12,64,512]{2,1,0:T(8,128)(2,1)S(1)}, bf16[12,64,512]{2,1,0:T(8,128)(2,1)}, u32[]{:S(2)}) copy-start(bf16[12,64,512]{2,1,0:T(8,128)(2,1)} %copy-done.1) | copy-start | bytes 2359300 | tf_op jit(solution)/shard_map/while
  236.7 49.3 %copy-start.4 = (bf16[12,64,512]{2,1,0:T(8,128)(2,1)S(1)}, bf16[12,64,512]{2,1,0:T(8,128)(2,1)}, u32[]{:S(2)}) copy-start(bf16[12,64,512]{2,1,0:T(8,128)(2,1)} %copy-done.3) | copy-start | bytes 2359300 | tf_op jit(solution)/shard_map/while
  236.7 49.3 %copy-start.8 = (s32[12,27]{1,0:T(8,128)S(1)}, s32[12,27]{1,0:T(8,128)}, u32[]{:S(2)}) copy-start(s32[12,27]{1,0:T(8,128)} %copy-done.7) | copy-start | bytes 3892 | tf_op jit(solution)/shard_map/while
  236.7 49.3 %copy-start.11 = (s32[4]{0:T(128)S(1)}, s32[4]{0:T(128)}, u32[]{:S(2)}) copy-start(s32[4]{0:T(128)} %copy-done.10) | copy-start | bytes 52 | tf_op jit(solution)/shard_map/while
  603.9 49.0 %copy-start.2 = (bf16[12,64,512]{2,1,0:T(8,128)(2,1)S(1)}, bf16[12,64,512]{2,1,0:T(8,128)(2,1)}, u32[]{:S(2)}) copy-start(bf16[12,64,512]{2,1,0:T(8,128)(2,1)} %copy-done.1) | copy-start | bytes 2359300 | tf_op jit(solution)/shard_map/while
  603.9 49.0 %copy-start.4 = (bf16[12,64,512]{2,1,0:T(8,128)(2,1)S(1)}, bf16[12,64,512]{2,1,0:T(8,128)(2,1)}, u32[]{:S(2)}) copy-start(bf16[12,64,512]{2,1,0:T(8,128)(2,1)} %copy-done.3) | copy-start | bytes 2359300 | tf_op jit(solution)/shard_map/while
  603.9 49.1 %copy-start.8 = (s32[12,27]{1,0:T(8,128)S(1)}, s32[12,27]{1,0:T(8,128)}, u32[]{:S(2)}) copy-start(s32[12,27]{1,0:T(8,128)} %copy-done.7) | copy-start | bytes 3892 | tf_op jit(solution)/shard_map/while
  603.9 49.1 %copy-start.11 = (s32[4]{0:T(128)S(1)}, s32[4]{0:T(128)}, u32[]{:S(2)}) copy-start(s32[4]{0:T(128)} %copy-done.10) | copy-start | bytes 52 | tf_op jit(solution)/shard_map/while
  787.5 48.9 %copy-start.4 = (bf16[12,64,512]{2,1,0:T(8,128)(2,1)S(1)}, bf16[12,64,512]{2,1,0:T(8,128)(2,1)}, u32[]{:S(2)}) copy-start(bf16[12,64,512]{2,1,0:T(8,128)(2,1)} %copy-done.3) | copy-start | bytes 2359300 | tf_op jit(solution)/shard_map/while
  787.5 48.9 %copy-start.8 = (s32[12,27]{1,0:T(8,128)S(1)}, s32[12,27]{1,0:T(8,128)}, u32[]{:S(2)}) copy-start(s32[12,27]{1,0:T(8,128)} %copy-done.7) | copy-start | bytes 3892 | tf_op jit(solution)/shard_map/while
  787.5 48.9 %copy-start.11 = (s32[4]{0:T(128)S(1)}, s32[4]{0:T(128)}, u32[]{:S(2)}) copy-start(s32[4]{0:T(128)} %copy-done.10) | copy-start | bytes 52 | tf_op jit(solution)/shard_map/while
  836.6 24.0 %all-to-all-start.4 = ((bf16[4,192,512]{2,1,0:T(8,128)(2,1)}), bf16[4,192,512]{2,1,0:T(8,128)(2,1)S(1)}, u32[]{:S(2)}, u32[]{:S(2)}) async-start(bf16[4,192,512]{2,1,0:T(8,128)(2,1)} %bitcast.157), calls=%async_computation.4 | async-start | bytes 1572864 | tf_op jit(solution)/shard_map/all_to_all | solution.py:174
  846.4 22.0 %collective-permute-start.2 = (bf16[12,64,1024]{2,1,0:T(8,128)(2,1)}, bf16[12,64,1024]{2,1,0:T(8,128)(2,1)}, u32[]{:S(2)}, u32[]{:S(2)}) collective-permute-start(bf16[12,64,1024]{2,1,0:T(8,128)(2,1)} %get-tuple-element.132), channel_id=1, source_target_pairs={{0,4},{4,8},{8,12},{12,16},{16,20},{20,24},{24,28},{1,5},{5,9},{9,... | collective-permute-start | bytes 4718600 | tf_op jit(solution)/shard_map/ppermute | solution.py:38
  852.5 36.4 %collective-permute-start.3 = (bf16[12,64,1024]{2,1,0:T(8,128)(2,1)S(1)}, bf16[12,64,1024]{2,1,0:T(8,128)(2,1)}, u32[]{:S(2)}, u32[]{:S(2)}) collective-permute-start(bf16[12,64,1024]{2,1,0:T(8,128)(2,1)S(1)} %get-tuple-element.133), channel_id=1, source_target_pairs={{4,0},{8,4},{12,8},{16,12},{20,16},{24,20},{28,24},{5,1},{9,5},{13... | collective-permute-start | bytes 4718600 | tf_op jit(solution)/shard_map/ppermute | solution.py:38
  860.7 33.0 %all-to-all-start.5 = ((bf16[4,192,512]{2,1,0:T(8,128)(2,1)}), bf16[4,192,512]{2,1,0:T(8,128)(2,1)S(1)}, u32[]{:S(2)}, u32[]{:S(2)}) async-start(bf16[4,192,512]{2,1,0:T(8,128)(2,1)} %bitcast.156), calls=%async_computation.5 | async-start | bytes 1572864 | tf_op jit(solution)/shard_map/all_to_all | solution.py:175
  919.6 23.4 %all-to-all-start.7 = ((bf16[4,192,512]{2,1,0:T(8,128)(2,1)}), bf16[4,192,512]{2,1,0:T(8,128)(2,1)S(1)}, u32[]{:S(2)}, u32[]{:S(2)}) async-start(bf16[4,192,512]{2,1,0:T(8,128)(2,1)} %bitcast.150), calls=%async_computation.7 | async-start | bytes 1572864 | tf_op jit(solution)/shard_map/all_to_all | solution.py:177
  (42 other events, 457.8 us)
where the time goes:
time: 949 us; the launch traced here: 944 us
  local copies, waits for them, and re-layouts  385 us (41%)
  other arithmetic  314 us (33%)
  waiting for transfers between devices  110 us (12%)
  matrix products  66.1 us (7%)
  starting transfers between devices  38.7 us (4%)
  blocking collectives  25.9 us (3%)
    scatter-add x4, other arithmetic, own_step(): grad_buffer.at[index_blk]  196 us
    concatenate x8, local copies, waits for them, and re-layouts, pair_grads(): jnp.concatenate([grad_key.reshape(block_tiles, key_len, -1), grad_value.r...  105 us
    gather x8, local copies, waits for them, and re-layouts, near_pairs(): jnp.take(pair_tiles, index_blk, axis=0)  90.7 us
    concatenate x4, other arithmetic, pair_grads(): jnp.concatenate([grad_key.reshape(block_tiles, key_len, -1), grad_value.r...  62.4 us
    transpose x4, local copies, waits for them, and re-layouts, pair_grads(): jnp.einsum('bntk,btnd->bknd', probs_low, cot_heads, preferred_element_typ...  53.1 us
    transpose x4, local copies, waits for them, and re-layouts, pair_grads(): jnp.einsum('bntk,btnd->bknd', grad_score, query_heads, preferred_element_...  53.1 us
    select_n x4, other arithmetic, near_pairs(): jnp.take(pair_tiles, index_blk, axis=0)  39.2 us
    slice x4, local copies, waits for them, and re-layouts, attend_both(): value_heads = split_heads(kv_near[:, :, feature_width:], head_count)  35.7 us
  transfers between devices with their start and end apart: 11, of which 9 were waited for; matrix products, arithmetic and copies ran while one was open for 3% of the time, Pallas kernels for 0%

commit v1 on v0

v1 whole, which is shorter than its diff:
```python
import functools
import math

import jax
import jax.numpy as jnp
from jax import lax
from jax.experimental import pallas as pl
from jax.experimental.pallas import tpu as pltpu
from jax.sharding import PartitionSpec as P

TILE = 64
TILE_ROWS = 3
TILE_COLS = 4
TILES_F = 12
HD = 128
FRAME = TILE * TILES_F
ROW = TILE * TILE_COLS
MESH = pl.DeviceIdType.MESH
masked_score = -1e30
F32 = jnp.float32
BF16 = jnp.bfloat16

NT = (((1,), (1,)), ((), ()))
TN = (((0,), (0,)), ((), ()))
NN = (((1,), (0,)), ((), ()))


def dot(a, b, dims):
    return lax.dot_general(a, b, dims, preferred_element_type=F32)


def kernel(
    nseq, nz, heads, rows,
    k_in, v_in, q_in, c_in, bias_ref,
    o_out, gq_out, gk_out, gv_out,
    kx, vx, qb, cb, o_st, gq_st, gk_st, gv_st, g_out, g_in, s_buf, gk_acc, gv_acc,
    in_send, in_recv, in_loc, halo_send, halo_recv, g_send, g_recv, out_send, out_recv, out_loc,
):
    s = lax.axis_index("seq")
    z = lax.axis_index("head")
    has_prev = s > 0
    has_next = s < nseq - 1
    scale = 1.0 / math.sqrt(HD)
    log2_scale = scale * math.log2(math.e)

    peers = [lax.rem(z + d, nz) for d in range(1, nz)]
    ins = (k_in, v_in, q_in, c_in)
    outs = (o_out, gq_out, gk_out, gv_out)
    stages = (o_st, gq_st, gk_st, gv_st)

    def in_place(a, h, source):
        if a < 2:
            start = FRAME + source * rows
            return (kx, vx)[a].at[h, pl.ds(pl.multiple_of(start, 32), rows), :]
        return (qb, cb)[a - 2].at[h, pl.ds(pl.multiple_of(source * rows, 32), rows), :]

    def columns(owner, h):
        return pl.ds(pl.multiple_of((owner * heads + h) * HD, HD), HD)

    def in_copy(a, h, peer, source):
        return pltpu.make_async_remote_copy(
            src_ref=ins[a].at[:, columns(peer, h)],
            dst_ref=in_place(a, h, source),
            send_sem=in_send.at[a, h, peer],
            recv_sem=in_recv.at[a, h, source],
            device_id=(s, peer),
            device_id_type=MESH,
        )

    def in_local(a, h):
        return pltpu.make_async_copy(
            ins[a].at[:, columns(z, h)], in_place(a, h, z), in_loc.at[a, h]
        )

    def out_copy(a, h, peer, source):
        return pltpu.make_async_remote_copy(
            src_ref=stages[a].at[h, pl.ds(pl.multiple_of(peer * rows, 32), rows), :],
            dst_ref=outs[a].at[:, columns(source, h)],
            send_sem=out_send.at[a, h, peer],
            recv_sem=out_recv.at[a, h, source],
            device_id=(s, peer),
            device_id_type=MESH,
        )

    def out_local(a, h):
        return pltpu.make_async_copy(
            stages[a].at[h, pl.ds(pl.multiple_of(z * rows, 32), rows), :],
            outs[a].at[:, columns(z, h)],
            out_loc.at[a, h],
        )

    def halo_copy(a, h, side):
        ext = (kx, vx)[a]
        return pltpu.make_async_remote_copy(
            src_ref=ext.at[h, pl.ds(FRAME, FRAME), :],
            dst_ref=ext.at[h, pl.ds(2 * FRAME * side, FRAME), :],
            send_sem=halo_send.at[a, h, side],
            recv_sem=halo_recv.at[a, h, side],
            device_id=(s + 1 - 2 * side, z),
            device_id_type=MESH,
        )

    def grad_copy(a, h, side):
        return pltpu.make_async_remote_copy(
            src_ref=g_out.at[a, h, side],
            dst_ref=g_in.at[a, h, side],
            send_sem=g_send.at[a, h, side],
            recv_sem=g_recv.at[a, h, side],
            device_id=(s - 1 + 2 * side, z),
            device_id_type=MESH,
        )

    barrier = pltpu.get_barrier_semaphore()
    for peer in peers:
        pl.semaphore_signal(barrier, inc=1, device_id=(s, peer), device_id_type=MESH)

    @pl.when(has_prev)
    def _():
        pl.semaphore_signal(barrier, inc=1, device_id=(s - 1, z), device_id_type=MESH)

    @pl.when(has_next)
    def _():
        pl.semaphore_signal(barrier, inc=1, device_id=(s + 1, z), device_id_type=MESH)

    pl.semaphore_wait(barrier, nz - 1 + has_prev.astype(jnp.int32) + has_next.astype(jnp.int32))

    def start_in(h, _):
        for a in range(4):
            for peer in peers:
                in_copy(a, h, peer, z).start()
            in_local(a, h).start()
        return 0

    lax.fori_loop(0, heads, start_in, 0)

    @pl.when(jnp.logical_not(has_prev))
    def _():
        kx[:, 0:FRAME, :] = jnp.zeros((heads, FRAME, HD), BF16)
        vx[:, 0:FRAME, :] = jnp.zeros((heads, FRAME, HD), BF16)

    @pl.when(jnp.logical_not(has_next))
    def _():
        kx[:, 2 * FRAME : 3 * FRAME, :] = jnp.zeros((heads, FRAME, HD), BF16)
        vx[:, 2 * FRAME : 3 * FRAME, :] = jnp.zeros((heads, FRAME, HD), BF16)

    def wait_in(h, arrays):
        for a in arrays:
            for peer in peers:
                in_copy(a, h, peer, peer).wait_recv()
            in_local(a, h).wait()

    def forward(h):
        wait_in(h, (0, 1))
        for side, there in ((0, has_next), (1, has_prev)):
            @pl.when(there)
            def _(side=side):
                for a in range(2):
                    halo_copy(a, h, side).start()

    def attend(h, r):
        low, high = max(r - 1, 0), min(r + 1, TILE_ROWS - 1)
        near = range(low, high + 1)
        base = r * ROW
        q = qb[h, base : base + ROW, :]
        c = cb[h, base : base + ROW, :]

        def first(f, top):
            for n in near:
                start = pl.multiple_of(f * FRAME + n * ROW, ROW)
                t = dot(kx[h, pl.ds(start, ROW), :], q, NT) * log2_scale
                rows_bias = bias_ref[r, f * TILE_ROWS + n]
                parts = []
                for k in range(TILE_COLS):
                    part = t[k * TILE : (k + 1) * TILE, :] + rows_bias[k : k + 1, :]
                    s_buf[pl.ds(start + k * TILE, TILE), :] = part
                    top = jnp.maximum(top, jnp.max(part.reshape(TILE // 8, 8, ROW), axis=0))
            return top

        top = lax.fori_loop(0, 3, first, jnp.full((8, ROW), masked_score, F32))
        top = jnp.max(top, axis=0, keepdims=True)

        def second(f, carry):
            total, out_t = carry
            for n in near:
                start = pl.multiple_of(f * FRAME + n * ROW, ROW)
                e = jnp.exp2(s_buf[pl.ds(start, ROW), :] - top)
                s_buf[pl.ds(start, ROW), :] = e
                total = total + jnp.sum(e.reshape(ROW // 8, 8, ROW), axis=0)
                out_t = out_t + dot(vx[h, pl.ds(start, ROW), :], e.astype(BF16), TN)
            return total, out_t

        total, out_t = lax.fori_loop(
            0, 3, second, (jnp.zeros((8, ROW), F32), jnp.zeros((HD, ROW), F32))
        )
        inverse = 1.0 / jnp.sum(total, axis=0, keepdims=True)
        out = jnp.transpose(out_t * inverse).astype(BF16)
        o_st[h, base : base + ROW, :] = out
        products = jnp.transpose(out.astype(F32) * c.astype(F32))
        grad_dot = jnp.sum(products, axis=0, keepdims=True)
        inverse_scaled = inverse * scale

        def third(f, gq_t):
            for n in near:
                start = pl.multiple_of(f * FRAME + n * ROW, ROW)
                here = pl.ds(start, ROW)
                e = s_buf[here, :]
                gp = dot(vx[h, here, :], c, NT)
                p_low = (e * inverse).astype(BF16)
                gs = ((e * inverse_scaled) * (gp - grad_dot)).astype(BF16)
                gv = dot(p_low, c, NN)
                gk = dot(gs, q, NN)
                if r == max(n - 1, 0):
                    gv_acc[here, :] = gv
                    gk_acc[here, :] = gk
                else:
                    gv_acc[here, :] += gv
                    gk_acc[here, :] += gk
                gq_t = gq_t + dot(kx[h, here, :], gs, TN)
            return gq_t

        gq_t = lax.fori_loop(0, 3, third, jnp.zeros((HD, ROW), F32))
        gq_st[h, base : base + ROW, :] = jnp.transpose(gq_t).astype(BF16)

    def send_out(a, h):
        for peer in peers:
            out_copy(a, h, peer, z).start()
        out_local(a, h).start()

    def finish(h):
        for side, there in ((1, has_prev), (0, has_next)):
            @pl.when(there)
            def _(side=side):
                for a in range(2):
                    grad_copy(a, h, side).wait_recv()
                    acc = (gk_acc, gv_acc)[a]
                    acc[FRAME : 2 * FRAME, :] += g_in[a, h, side].astype(F32)
        for a in range(2):
            stages[2 + a][h] = (gk_acc, gv_acc)[a][FRAME : 2 * FRAME, :].astype(BF16)
            send_out(2 + a, h)

    forward(0)

    def one_head(h, _):
        wait_in(h, (2, 3))
        for side, there in ((0, has_prev), (1, has_next)):
            @pl.when(there)
            def _(side=side):
                for a in range(2):
                    halo_copy(a, h, side).wait_recv()

        @pl.when(h > 0)
        def _():
            finish(h - 1)

        for r in range(TILE_ROWS):
            attend(h, r)
        for side, there in ((0, has_prev), (1, has_next)):
            @pl.when(there)
            def _(side=side):
                for a in range(2):
                    part = (gk_acc, gv_acc)[a][pl.ds(2 * FRAME * side, FRAME), :]
                    g_out[a, h, side] = part.astype(BF16)
                    grad_copy(a, h, side).start()
        send_out(0, h)
        send_out(1, h)

        @pl.when(h + 1 < heads)
        def _():
            forward(h + 1)

        return 0

    lax.fori_loop(0, heads, one_head, 0)
    finish(heads - 1)

    def drain(h, _):
        for a in range(4):
            for peer in peers:
                in_copy(a, h, peer, z).wait_send()
                out_copy(a, h, peer, z).wait_send()
                out_copy(a, h, peer, peer).wait_recv()
            out_local(a, h).wait()
        for a in range(2):
            for side, there, back in ((0, has_next, has_prev), (1, has_prev, has_next)):
                @pl.when(there)
                def _(a=a, side=side):
                    halo_copy(a, h, side).wait_send()

                @pl.when(back)
                def _(a=a, side=side):
                    grad_copy(a, h, side).wait_send()
        return 0

    lax.fori_loop(0, heads, drain, 0)


def shards(nseq, nz, queries, keys, values, cotangent, neighbours):
    rows, width = queries.shape
    heads = width // HD // nz
    first_tile = lax.axis_index("seq") * TILES_F
    listed = lax.dynamic_slice_in_dim(neighbours, first_tile, TILES_F, 0)
    relative = jnp.where(listed >= 0, listed - (first_tile - TILES_F), -1)
    near = jnp.arange(3 * TILES_F, dtype=jnp.int32)
    present = jnp.any(relative[:, :, None] == near[None, None, :], axis=1)
    bias = jnp.where(present, 0.0, masked_score).astype(F32)
    bias = bias.reshape(TILE_ROWS, TILE_COLS, 3 * TILE_ROWS, TILE_COLS).transpose(0, 2, 3, 1)
    bias = jnp.repeat(bias, TILE, axis=3)
    bias = jnp.pad(bias, ((0, 0), (0, 0), (0, 8 - TILE_COLS), (0, 0)))
    vmem = pl.BlockSpec(memory_space=pltpu.VMEM)
    dma = pltpu.SemaphoreType.DMA
    return pl.pallas_call(
        functools.partial(kernel, nseq, nz, heads, rows),
        out_shape=[jax.ShapeDtypeStruct((rows, width), BF16)] * 4,
        in_specs=[vmem] * 5,
        out_specs=[vmem] * 4,
        scratch_shapes=[
            pltpu.VMEM((heads, 3 * FRAME, HD), BF16),
            pltpu.VMEM((heads, 3 * FRAME, HD), BF16),
            pltpu.VMEM((heads, FRAME, HD), BF16),
            pltpu.VMEM((heads, FRAME, HD), BF16),
            pltpu.VMEM((heads, FRAME, HD), BF16),
            pltpu.VMEM((heads, FRAME, HD), BF16),
            pltpu.VMEM((heads, FRAME, HD), BF16),
            pltpu.VMEM((heads, FRAME, HD), BF16),
            pltpu.VMEM((2, heads, 2, FRAME, HD), BF16),
            pltpu.VMEM((2, heads, 2, FRAME, HD), BF16),
            pltpu.VMEM((3 * FRAME, ROW), F32),
            pltpu.VMEM((3 * FRAME, HD), F32),
            pltpu.VMEM((3 * FRAME, HD), F32),
            dma((4, heads, nz)),
            dma((4, heads, nz)),
            dma((4, heads)),
            dma((2, heads, 2)),
            dma((2, heads, 2)),
            dma((2, heads, 2)),
            dma((2, heads, 2)),
            dma((4, heads, nz)),
            dma((4, heads, nz)),
            dma((4, heads)),
        ],
        compiler_params=pltpu.CompilerParams(
            collective_id=0, has_side_effects=True, vmem_limit_bytes=56 * 1024 * 1024
        ),
    )(keys, values, queries, cotangent, bias)


def solution(mesh):
    placed = P(("seq", "head"), None)
    return jax.shard_map(
        functools.partial(shards, mesh.shape["seq"], mesh.shape["head"]),
        mesh=mesh,
        in_specs=(placed, placed, placed, placed, P()),
        out_specs=(placed, placed, placed, placed),
        check_vma=False,
    )
```

time: 949 us -> 157 us (0.17)
  local copies, waits for them, and re-layouts: 385 us -> 7.92 us
  other arithmetic: 314 us -> 0.22 us
  Pallas kernels: 0 us -> 146 us
  waiting for transfers between devices: 110 us -> 0 us
  matrix products: 66.1 us -> 0 us
  starting transfers between devices: 38.7 us -> 0 us
  blocking collectives: 25.9 us -> 0 us
    scatter-add x4 -> x0, other arithmetic: 196 us -> none  [own_step(): grad_buffer.at[index_blk]]
    pallas_call x0 -> x1, Pallas kernels: none -> 146 us  [shards(): pl.pallas_call(functools.partial(kernel, nseq, nz, heads, rows), out_shap...]
    concatenate x9 -> x0, local copies, waits for them, and re-layouts: 108 us -> none  [the longest x8 105 us: pair_grads(): jnp.concatenate([grad_key.reshape(block_tiles, key_len, -1), grad_value.r...]
    transpose x8 -> x1, local copies, waits for them, and re-layouts: 106 us -> 0.02 us  [shards(): bias.reshape(TILE_ROWS, TILE_COLS, 3 * TILE_ROWS, TILE_COLS)]
    gather x9 -> x0, local copies, waits for them, and re-layouts: 91.2 us -> none  [the longest x8 90.7 us: near_pairs(): jnp.take(pair_tiles, index_blk, axis=0)]
    all_to_all x7 -> x0, waiting for transfers between devices: 74.1 us -> none  [the longest x1 18.6 us: shards(): lax.all_to_all(values, 'head', split_axis=1, concat_axis=0, tiled=True)]
    concatenate x6 -> x0, other arithmetic: 66.5 us -> none  [the longest x4 62.4 us: pair_grads(): jnp.concatenate([grad_key.reshape(block_tiles, key_len, -1), grad_value.r...]
    dot_general x24 -> x0, matrix products: 66.1 us -> none  [the longest x4 16.6 us: tile_probs(): jnp.einsum('btnd,bknd->bntk', query_heads, key_heads, preferred_element_t...]
  transfers between devices with their start and end apart: 11 -> 0, of which waited for: 9 -> 0; matrix products, arithmetic and copies ran while one was open for 3% -> 0% of each run, Pallas kernels for 0% -> 0%
where the time goes in v1:
time: 157 us; the launch traced here: 155 us
  Pallas kernels  146 us (93%)
  local copies, waits for them, and re-layouts  7.92 us (5%)
    pallas_call x1, Pallas kernels, shards(): pl.pallas_call(functools.partial(kernel, nseq, nz, heads, rows), out_shap...  146 us
    unnamed x12, local copies, waits for them, and re-layouts  6.58 us

profile of v1, /device:TPU:2, one launch (start us, length us, event | category | flops | bytes accessed | tf_op | source)
XLA Modules:
  0.0 154.9 jit_solution(5557129600379620786)
XLA Ops:
  0.6 0.0 copy-start.3
  0.6 0.7 copy-done.3
  1.3 0.1 subtract_select_fusion
  1.4 0.1 copy.12
  1.5 0.1 fusion
  1.7 0.1 copy.13
  1.8 0.1 select_n.18
  1.9 0.2 broadcast_in_dim.20
  2.1 0.2 reshape.17
  2.2 0.7 pad.4.bias_ref
  2.9 146.0 %shard_map.84 = (bf16[192,2048]{1,0:T(8,128)(2,1)}, bf16[192,2048]{1,0:T(8,128)(2,1)}, bf16[192,2048]{1,0:T(8,128)(2,1)}, bf16[192,2048]{1,0:T(8,128)(2,1)}) custom-call(bf16[192,2048]{1,0:T(8,128)(2,1)} %k_in.1, bf16[192,2048]{1,0:T(8,128)(2,1)} %v_in.1, bf16[192,2048]{1,0:T(8,128)(2,1)} %q_in.1, bf16[192,2048]{1,0:T(8,128)(2,1)} %c_in.1, ...), custom_call_target="tpu_custom_call" | custom-call | tf_op jit(solution)/shard_map/pallas_call | solution.py:311
  149.0 0.0 copy-start.2
  149.0 2.2 %copy.19 = bf16[192,2048]{1,0:T(8,128)(2,1)} copy(bf16[192,2048]{1,0:T(8,128)(2,1)} %get-tuple-element.8) | data formatting | bytes 1572864
  151.1 0.0 copy-done.2
  151.1 0.0 copy-start.1
  151.1 0.9 copy.20
  152.0 0.5 copy-done.1
  152.6 0.0 copy-start
  152.6 0.9 copy.21
  153.4 0.5 copy-done
  154.0 0.9 copy.22
  (2 shorter events, 0.0 us)
Async XLA Ops:
  0.6 0.7 copy-start.3
  149.0 2.2 %copy-start.2 = (bf16[192,2048]{1,0:T(8,128)(2,1)S(1)}, bf16[192,2048]{1,0:T(8,128)(2,1)}, u32[]{:S(2)}) copy-start(bf16[192,2048]{1,0:T(8,128)(2,1)} %get-tuple-element.9) | copy-start | bytes 2359300
  151.1 1.4 copy-start.1
  152.6 1.4 copy-start

commit v2 on v1

--- a/solution.py
+++ b/solution.py
@@ -31,9 +31,9 @@
 
 def kernel(
     nseq, nz, heads, rows,
-    k_in, v_in, q_in, c_in, bias_ref,
+    k_in, v_in, q_in, c_in, near_ref,
     o_out, gq_out, gk_out, gv_out,
-    kx, vx, qb, cb, o_st, gq_st, gk_st, gv_st, g_out, g_in, s_buf, gk_acc, gv_acc,
+    kx, vx, qb, cb, o_st, gq_st, gk_st, gv_st, g_out, g_in, s_buf, gk_acc, gv_acc, bias_ref,
     in_send, in_recv, in_loc, halo_send, halo_recv, g_send, g_recv, out_send, out_recv, out_loc,
 ):
     s = lax.axis_index("seq")
@@ -132,6 +132,26 @@
         return 0
 
     lax.fori_loop(0, heads, start_in, 0)
+
+    first_tile = s * TILES_F
+    ext_rows = 40
+    listed = near_ref[...]
+    count = listed.shape[1]
+    ext_row = lax.broadcasted_iota(jnp.int32, (ext_rows, count), 0)
+    present = jnp.zeros((ext_rows, count), F32)
+    for k in range(3 * TILES_F):
+        tile = first_tile - TILES_F + k
+        match = (listed == tile) & (listed >= 0)
+        match = jnp.max(jnp.where(match, 1.0, 0.0).astype(F32), axis=0, keepdims=True)
+        present = jnp.where(ext_row == k, match, present)
+    present = present.astype(BF16)
+    tile_row = lax.broadcasted_iota(jnp.int32, (count, ROW), 0)
+    lane_tile = first_tile + lax.broadcasted_iota(jnp.int32, (count, ROW), 1) // TILE
+    for r in range(TILE_ROWS):
+        spread = jnp.where(tile_row == lane_tile + r * TILE_COLS, 1.0, 0.0).astype(BF16)
+        bias = jnp.where(dot(present, spread, NN) > 0.5, 0.0, masked_score).astype(F32)
+        for n in range(3 * TILE_ROWS):
+            bias_ref[r, n, 0:TILE_COLS, :] = bias[n * TILE_COLS : (n + 1) * TILE_COLS, :]
 
     @pl.when(jnp.logical_not(has_prev))
     def _():
@@ -236,7 +256,6 @@
                     acc[FRAME : 2 * FRAME, :] += g_in[a, h, side].astype(F32)
         for a in range(2):
             stages[2 + a][h] = (gk_acc, gv_acc)[a][FRAME : 2 * FRAME, :].astype(BF16)
-            send_out(2 + a, h)
 
     forward(0)
 
@@ -251,6 +270,11 @@
         @pl.when(h > 0)
         def _():
             finish(h - 1)
+
+        @pl.when((h > 0) & (h == heads - 1))
+        def _():
+            send_out(2, h - 1)
+            send_out(3, h - 1)
 
         for r in range(TILE_ROWS):
             attend(h, r)
@@ -261,17 +285,37 @@
                     part = (gk_acc, gv_acc)[a][pl.ds(2 * FRAME * side, FRAME), :]
                     g_out[a, h, side] = part.astype(BF16)
                     grad_copy(a, h, side).start()
-        send_out(0, h)
-        send_out(1, h)
+
+        @pl.when(h == heads - 1)
+        def _():
+            send_out(0, h)
+            send_out(1, h)
 
         @pl.when(h + 1 < heads)
         def _():
             forward(h + 1)
 
+        @pl.when(h == heads - 2)
+        def _():
+            def flush(ready, _):
+                send_out(0, ready)
+                send_out(1, ready)
+
+                @pl.when(ready < heads - 2)
+                def _():
+                    send_out(2, ready)
+                    send_out(3, ready)
+
+                return 0
+
+            lax.fori_loop(0, heads - 1, flush, 0)
+
         return 0
 
     lax.fori_loop(0, heads, one_head, 0)
     finish(heads - 1)
+    send_out(2, heads - 1)
+    send_out(3, heads - 1)
 
     def drain(h, _):
         for a in range(4):
@@ -294,25 +338,25 @@
     lax.fori_loop(0, heads, drain, 0)
 
 
+def place_results(*refs):
+    done = refs[8]
+    copies = [pltpu.make_async_copy(refs[a], refs[4 + a], done.at[a]) for a in range(4)]
+    for copy in copies:
+        copy.start()
+    for copy in copies:
+        copy.wait()
+
+
 def shards(nseq, nz, queries, keys, values, cotangent, neighbours):
     rows, width = queries.shape
     heads = width // HD // nz
-    first_tile = lax.axis_index("seq") * TILES_F
-    listed = lax.dynamic_slice_in_dim(neighbours, first_tile, TILES_F, 0)
-    relative = jnp.where(listed >= 0, listed - (first_tile - TILES_F), -1)
-    near = jnp.arange(3 * TILES_F, dtype=jnp.int32)
-    present = jnp.any(relative[:, :, None] == near[None, None, :], axis=1)
-    bias = jnp.where(present, 0.0, masked_score).astype(F32)
-    bias = bias.reshape(TILE_ROWS, TILE_COLS, 3 * TILE_ROWS, TILE_COLS).transpose(0, 2, 3, 1)
-    bias = jnp.repeat(bias, TILE, axis=3)
-    bias = jnp.pad(bias, ((0, 0), (0, 0), (0, 8 - TILE_COLS), (0, 0)))
-    vmem = pl.BlockSpec(memory_space=pltpu.VMEM)
+    place = pl.BlockSpec(memory_space=pl.ANY)
     dma = pltpu.SemaphoreType.DMA
-    return pl.pallas_call(
+    results = pl.pallas_call(
         functools.partial(kernel, nseq, nz, heads, rows),
         out_shape=[jax.ShapeDtypeStruct((rows, width), BF16)] * 4,
-        in_specs=[vmem] * 5,
-        out_specs=[vmem] * 4,
+        in_specs=[place] * 4 + [pl.BlockSpec(memory_space=pltpu.VMEM)],
+        out_specs=[place] * 4,
         scratch_shapes=[
             pltpu.VMEM((heads, 3 * FRAME, HD), BF16),
             pltpu.VMEM((heads, 3 * FRAME, HD), BF16),
@@ -327,6 +371,7 @@
             pltpu.VMEM((3 * FRAME, ROW), F32),
             pltpu.VMEM((3 * FRAME, HD), F32),
             pltpu.VMEM((3 * FRAME, HD), F32),
+            pltpu.VMEM((TILE_ROWS, 3 * TILE_ROWS, 8, ROW), F32),
             dma((4, heads, nz)),
             dma((4, heads, nz)),
             dma((4, heads)),
@@ -341,7 +386,15 @@
         compiler_params=pltpu.CompilerParams(
             collective_id=0, has_side_effects=True, vmem_limit_bytes=56 * 1024 * 1024
         ),
-    )(keys, values, queries, cotangent, bias)
+    )(keys, values, queries, cotangent, neighbours.T)
+    return pl.pallas_call(
+        place_results,
+        out_shape=[jax.ShapeDtypeStruct((rows, width), BF16)] * 4,
+        in_specs=[place] * 4,
+        out_specs=[place] * 4,
+        scratch_shapes=[dma((4,))],
+        compiler_params=pltpu.CompilerParams(vmem_limit_bytes=56 * 1024 * 1024),
+    )(*results)
 
 
 def solution(mesh):

time: 157 us -> 260 us (1.66)
  the two profiles are of different devices: /device:TPU:2 before, /device:TPU:27 now
where the time goes in v2:
time: 260 us
  Pallas kernels  259 us (100%)
    pallas_call x1, Pallas kernels, shards(): pl.pallas_call(functools.partial(kernel, nseq, nz, heads, rows), out_shap...  163 us
    pallas_call x1, Pallas kernels, shards(): pl.pallas_call(place_results, out_shape=[jax.ShapeDtypeStruct((rows, widt...  96.4 us

profile of v2, /device:TPU:27, one launch (start us, length us, event | category | flops | bytes accessed | tf_op | source)
XLA Modules:
  0.0 259.9 jit_solution(17801171995250112913)
XLA Ops:
  0.6 162.8 %shard_map.84 = (bf16[192,2048]{1,0:T(8,128)(2,1)}, bf16[192,2048]{1,0:T(8,128)(2,1)}, bf16[192,2048]{1,0:T(8,128)(2,1)}, bf16[192,2048]{1,0:T(8,128)(2,1)}) custom-call(bf16[192,2048]{1,0:T(8,128)(2,1)} %k_in.1, bf16[192,2048]{1,0:T(8,128)(2,1)} %v_in.1, bf16[192,2048]{1,0:T(8,128)(2,1)} %q_in.1, bf16[192,2048]{1,0:T(8,128)(2,1)} %c_in.1, s32[27,96]{1,0:T(8,128)} %bitcast.1), custom_call_target="tpu_custom_call" | custom-call | tf_op jit(solution)/shard_map/pallas_call | solution.py:355
  163.5 96.4 %shard_map.85 = (bf16[192,2048]{1,0:T(8,128)(2,1)}, bf16[192,2048]{1,0:T(8,128)(2,1)}, bf16[192,2048]{1,0:T(8,128)(2,1)}, bf16[192,2048]{1,0:T(8,128)(2,1)}) custom-call(bf16[192,2048]{1,0:T(8,128)(2,1)} %get-tuple-element.8.refs_0_, bf16[192,2048]{1,0:T(8,128)(2,1)} %get-tuple-element.9.refs_1_, bf16[192,2048]{1,0:T(8,128)(2,1)} %get-tuple-element.10.refs_2_, ...), custom_call_target="tpu_custom_call" | custom-call | tf_op jit(solution)/shard_map/pallas_call | solution.py:390

commit v3 on v2

--- a/solution.py
+++ b/solution.py
@@ -339,24 +339,20 @@
 
 
 def place_results(*refs):
-    done = refs[8]
-    copies = [pltpu.make_async_copy(refs[a], refs[4 + a], done.at[a]) for a in range(4)]
-    for copy in copies:
-        copy.start()
-    for copy in copies:
-        copy.wait()
+    for a in range(4):
+        refs[4 + a][...] = refs[a][...]
 
 
 def shards(nseq, nz, queries, keys, values, cotangent, neighbours):
     rows, width = queries.shape
     heads = width // HD // nz
-    place = pl.BlockSpec(memory_space=pl.ANY)
+    vmem = pl.BlockSpec(memory_space=pltpu.VMEM)
     dma = pltpu.SemaphoreType.DMA
     results = pl.pallas_call(
         functools.partial(kernel, nseq, nz, heads, rows),
         out_shape=[jax.ShapeDtypeStruct((rows, width), BF16)] * 4,
-        in_specs=[place] * 4 + [pl.BlockSpec(memory_space=pltpu.VMEM)],
-        out_specs=[place] * 4,
+        in_specs=[vmem] * 5,
+        out_specs=[vmem] * 4,
         scratch_shapes=[
             pltpu.VMEM((heads, 3 * FRAME, HD), BF16),
             pltpu.VMEM((heads, 3 * FRAME, HD), BF16),
@@ -387,12 +383,14 @@
             collective_id=0, has_side_effects=True, vmem_limit_bytes=56 * 1024 * 1024
         ),
     )(keys, values, queries, cotangent, neighbours.T)
+    block_rows = 48 if rows % 48 == 0 else rows
+    block = pl.BlockSpec((block_rows, width), lambda i: (i, 0))
     return pl.pallas_call(
         place_results,
+        grid=(rows // block_rows,),
         out_shape=[jax.ShapeDtypeStruct((rows, width), BF16)] * 4,
-        in_specs=[place] * 4,
-        out_specs=[place] * 4,
-        scratch_shapes=[dma((4,))],
+        in_specs=[block] * 4,
+        out_specs=[block] * 4,
         compiler_params=pltpu.CompilerParams(vmem_limit_bytes=56 * 1024 * 1024),
     )(*results)
 

time: 260 us -> 170 us (0.65)
  Pallas kernels: 259 us -> 170 us
    pallas_call x1, Pallas kernels: 96.4 us -> 4.24 us  [shards(): pl.pallas_call(place_results, grid=(rows // block_rows,), out_shape=[jax....]
where the time goes in v3:
time: 170 us
  Pallas kernels  170 us (100%)
    pallas_call x1, Pallas kernels, shards(): pl.pallas_call(functools.partial(kernel, nseq, nz, heads, rows), out_shap...  165 us
    pallas_call x1, Pallas kernels, shards(): pl.pallas_call(place_results, grid=(rows // block_rows,), out_shape=[jax....  4.24 us

profile of v3, /device:TPU:27, one launch (start us, length us, event | category | flops | bytes accessed | tf_op | source)
XLA Modules:
  0.0 170.1 jit_solution(1690468431683866945)
XLA Ops:
  0.6 165.3 %shard_map.84 = (bf16[192,2048]{1,0:T(8,128)(2,1)}, bf16[192,2048]{1,0:T(8,128)(2,1)}, bf16[192,2048]{1,0:T(8,128)(2,1)}, bf16[192,2048]{1,0:T(8,128)(2,1)}) custom-call(bf16[192,2048]{1,0:T(8,128)(2,1)} %k_in.1, bf16[192,2048]{1,0:T(8,128)(2,1)} %v_in.1, bf16[192,2048]{1,0:T(8,128)(2,1)} %q_in.1, bf16[192,2048]{1,0:T(8,128)(2,1)} %c_in.1, s32[27,96]{1,0:T(8,128)} %bitcast.1), custom_call_target="tpu_custom_call" | custom-call | tf_op jit(solution)/shard_map/pallas_call | solution.py:351
  165.9 4.2 %shard_map.85 = (bf16[192,2048]{1,0:T(8,128)(2,1)}, bf16[192,2048]{1,0:T(8,128)(2,1)}, bf16[192,2048]{1,0:T(8,128)(2,1)}, bf16[192,2048]{1,0:T(8,128)(2,1)}) custom-call(bf16[192,2048]{1,0:T(8,128)(2,1)} %get-tuple-element.8.refs_0_, bf16[192,2048]{1,0:T(8,128)(2,1)} %get-tuple-element.9.refs_1_, bf16[192,2048]{1,0:T(8,128)(2,1)} %get-tuple-element.10.refs_2_, ...), custom_call_target="tpu_custom_call" | custom-call | tf_op jit(solution)/shard_map/pallas_call | solution.py:388

commit v4 on v3

--- a/solution.py
+++ b/solution.py
@@ -124,14 +124,13 @@
 
     pl.semaphore_wait(barrier, nz - 1 + has_prev.astype(jnp.int32) + has_next.astype(jnp.int32))
 
-    def start_in(h, _):
+    def start_in(h):
         for a in range(4):
             for peer in peers:
                 in_copy(a, h, peer, z).start()
             in_local(a, h).start()
-        return 0
-
-    lax.fori_loop(0, heads, start_in, 0)
+
+    start_in(0)
 
     first_tile = s * TILES_F
     ext_rows = 40
@@ -177,6 +176,10 @@
                 for a in range(2):
                     halo_copy(a, h, side).start()
 
+        @pl.when(h + 1 < heads)
+        def _():
+            start_in(h + 1)
+
     def attend(h, r):
         low, high = max(r - 1, 0), min(r + 1, TILE_ROWS - 1)
         near = range(low, high + 1)
@@ -270,9 +273,6 @@
         @pl.when(h > 0)
         def _():
             finish(h - 1)
-
-        @pl.when((h > 0) & (h == heads - 1))
-        def _():
             send_out(2, h - 1)
             send_out(3, h - 1)
 
@@ -286,30 +286,12 @@
                     g_out[a, h, side] = part.astype(BF16)
                     grad_copy(a, h, side).start()
 
-        @pl.when(h == heads - 1)
-        def _():
-            send_out(0, h)
-            send_out(1, h)
-
         @pl.when(h + 1 < heads)
         def _():
             forward(h + 1)
 
-        @pl.when(h == heads - 2)
-        def _():
-            def flush(ready, _):
-                send_out(0, ready)
-                send_out(1, ready)
-
-                @pl.when(ready < heads - 2)
-                def _():
-                    send_out(2, ready)
-                    send_out(3, ready)
-
-                return 0
-
-            lax.fori_loop(0, heads - 1, flush, 0)
-
+        send_out(0, h)
+        send_out(1, h)
         return 0
 
     lax.fori_loop(0, heads, one_head, 0)

time: 170 us -> 153 us (0.900)
  the two profiles are of different devices: /device:TPU:27 before, /device:TPU:2 now
where the time goes in v4:
time: 153 us; the launch traced here: 151 us
  Pallas kernels  150 us (98%)
    pallas_call x1, Pallas kernels, shards(): pl.pallas_call(functools.partial(kernel, nseq, nz, heads, rows), out_shap...  146 us
    pallas_call x1, Pallas kernels, shards(): pl.pallas_call(place_results, grid=(rows // block_rows,), out_shape=[jax....  4.24 us

profile of v4, /device:TPU:2, one launch (start us, length us, event | category | flops | bytes accessed | tf_op | source)
XLA Modules:
  0.0 151.0 jit_solution(1113410773428541698)
XLA Ops:
  0.6 146.1 %shard_map.84 = (bf16[192,2048]{1,0:T(8,128)(2,1)}, bf16[192,2048]{1,0:T(8,128)(2,1)}, bf16[192,2048]{1,0:T(8,128)(2,1)}, bf16[192,2048]{1,0:T(8,128)(2,1)}) custom-call(bf16[192,2048]{1,0:T(8,128)(2,1)} %k_in.1, bf16[192,2048]{1,0:T(8,128)(2,1)} %v_in.1, bf16[192,2048]{1,0:T(8,128)(2,1)} %q_in.1, bf16[192,2048]{1,0:T(8,128)(2,1)} %c_in.1, s32[27,96]{1,0:T(8,128)} %bitcast.1), custom_call_target="tpu_custom_call" | custom-call | tf_op jit(solution)/shard_map/pallas_call | solution.py:333
  146.7 4.2 %shard_map.85 = (bf16[192,2048]{1,0:T(8,128)(2,1)}, bf16[192,2048]{1,0:T(8,128)(2,1)}, bf16[192,2048]{1,0:T(8,128)(2,1)}, bf16[192,2048]{1,0:T(8,128)(2,1)}) custom-call(bf16[192,2048]{1,0:T(8,128)(2,1)} %get-tuple-element.8.refs_0_, bf16[192,2048]{1,0:T(8,128)(2,1)} %get-tuple-element.9.refs_1_, bf16[192,2048]{1,0:T(8,128)(2,1)} %get-tuple-element.10.refs_2_, ...), custom_call_target="tpu_custom_call" | custom-call | tf_op jit(solution)/shard_map/pallas_call | solution.py:370

commit v5 on v4

--- a/solution.py
+++ b/solution.py
@@ -33,7 +33,7 @@
     nseq, nz, heads, rows,
     k_in, v_in, q_in, c_in, near_ref,
     o_out, gq_out, gk_out, gv_out,
-    kx, vx, qb, cb, o_st, gq_st, gk_st, gv_st, g_out, g_in, s_buf, gk_acc, gv_acc, bias_ref,
+    kx, vx, qb, cb, o_st, gq_st, gk_st, gv_st, g_out, g_in, s_buf, gk_acc, gv_acc, bias_ref, own,
     in_send, in_recv, in_loc, halo_send, halo_recv, g_send, g_recv, out_send, out_recv, out_loc,
 ):
     s = lax.axis_index("seq")
@@ -255,10 +255,9 @@
             def _(side=side):
                 for a in range(2):
                     grad_copy(a, h, side).wait_recv()
-                    acc = (gk_acc, gv_acc)[a]
-                    acc[FRAME : 2 * FRAME, :] += g_in[a, h, side].astype(F32)
+                    own[a] += g_in[a, h, side].astype(F32)
         for a in range(2):
-            stages[2 + a][h] = (gk_acc, gv_acc)[a][FRAME : 2 * FRAME, :].astype(BF16)
+            stages[2 + a][h] = own[a].astype(BF16)
 
     forward(0)
 
@@ -270,14 +269,22 @@
                 for a in range(2):
                     halo_copy(a, h, side).wait_recv()
 
+        attend(h, 0)
+        attend(h, 1)
+
+        @pl.when(h + 1 < heads)
+        def _():
+            forward(h + 1)
+
         @pl.when(h > 0)
         def _():
             finish(h - 1)
             send_out(2, h - 1)
             send_out(3, h - 1)
 
-        for r in range(TILE_ROWS):
-            attend(h, r)
+        attend(h, 2)
+        for a in range(2):
+            own[a] = (gk_acc, gv_acc)[a][FRAME : 2 * FRAME, :]
         for side, there in ((0, has_prev), (1, has_next)):
             @pl.when(there)
             def _(side=side):
@@ -285,10 +292,6 @@
                     part = (gk_acc, gv_acc)[a][pl.ds(2 * FRAME * side, FRAME), :]
                     g_out[a, h, side] = part.astype(BF16)
                     grad_copy(a, h, side).start()
-
-        @pl.when(h + 1 < heads)
-        def _():
-            forward(h + 1)
 
         send_out(0, h)
         send_out(1, h)
@@ -328,13 +331,13 @@
 def shards(nseq, nz, queries, keys, values, cotangent, neighbours):
     rows, width = queries.shape
     heads = width // HD // nz
-    vmem = pl.BlockSpec(memory_space=pltpu.VMEM)
+    place = pl.BlockSpec(memory_space=pl.ANY)
     dma = pltpu.SemaphoreType.DMA
     results = pl.pallas_call(
         functools.partial(kernel, nseq, nz, heads, rows),
         out_shape=[jax.ShapeDtypeStruct((rows, width), BF16)] * 4,
-        in_specs=[vmem] * 5,
-        out_specs=[vmem] * 4,
+        in_specs=[place] * 4 + [pl.BlockSpec(memory_space=pltpu.VMEM)],
+        out_specs=[place] * 4,
         scratch_shapes=[
             pltpu.VMEM((heads, 3 * FRAME, HD), BF16),
             pltpu.VMEM((heads, 3 * FRAME, HD), BF16),
@@ -350,6 +353,7 @@
             pltpu.VMEM((3 * FRAME, HD), F32),
             pltpu.VMEM((3 * FRAME, HD), F32),
             pltpu.VMEM((TILE_ROWS, 3 * TILE_ROWS, 8, ROW), F32),
+            pltpu.VMEM((2, FRAME, HD), F32),
             dma((4, heads, nz)),
             dma((4, heads, nz)),
             dma((4, heads)),

time: 153 us -> 150 us (0.980)
  Pallas kernels: 150 us -> 148 us
    pallas_call x1, Pallas kernels: 146 us -> 144 us  [shards(): pl.pallas_call(functools.partial(kernel, nseq, nz, heads, rows), out_shap...]
where the time goes in v5:
time: 150 us; the launch traced here: 148 us
  Pallas kernels  148 us (99%)
    pallas_call x1, Pallas kernels, shards(): pl.pallas_call(functools.partial(kernel, nseq, nz, heads, rows), out_shap...  144 us
    pallas_call x1, Pallas kernels, shards(): pl.pallas_call(place_results, grid=(rows // block_rows,), out_shape=[jax....  4.24 us

profile of v5, /device:TPU:2, one launch (start us, length us, event | category | flops | bytes accessed | tf_op | source)
XLA Modules:
  0.0 148.5 jit_solution(15485616402859923166)
XLA Ops:
  0.6 143.6 %shard_map.84 = (bf16[192,2048]{1,0:T(8,128)(2,1)}, bf16[192,2048]{1,0:T(8,128)(2,1)}, bf16[192,2048]{1,0:T(8,128)(2,1)}, bf16[192,2048]{1,0:T(8,128)(2,1)}) custom-call(bf16[192,2048]{1,0:T(8,128)(2,1)} %k_in.1, bf16[192,2048]{1,0:T(8,128)(2,1)} %v_in.1, bf16[192,2048]{1,0:T(8,128)(2,1)} %q_in.1, bf16[192,2048]{1,0:T(8,128)(2,1)} %c_in.1, s32[27,96]{1,0:T(8,128)} %bitcast.1), custom_call_target="tpu_custom_call" | custom-call | tf_op jit(solution)/shard_map/pallas_call | solution.py:336
  144.2 4.2 %shard_map.85 = (bf16[192,2048]{1,0:T(8,128)(2,1)}, bf16[192,2048]{1,0:T(8,128)(2,1)}, bf16[192,2048]{1,0:T(8,128)(2,1)}, bf16[192,2048]{1,0:T(8,128)(2,1)}) custom-call(bf16[192,2048]{1,0:T(8,128)(2,1)} %get-tuple-element.8.refs_0_, bf16[192,2048]{1,0:T(8,128)(2,1)} %get-tuple-element.9.refs_1_, bf16[192,2048]{1,0:T(8,128)(2,1)} %get-tuple-element.10.refs_2_, ...), custom_call_target="tpu_custom_call" | custom-call | tf_op jit(solution)/shard_map/pallas_call | solution.py:374

commit v6 on v5

--- a/solution.py
+++ b/solution.py
@@ -75,7 +75,7 @@
     def out_copy(a, h, peer, source):
         return pltpu.make_async_remote_copy(
             src_ref=stages[a].at[h, pl.ds(pl.multiple_of(peer * rows, 32), rows), :],
-            dst_ref=outs[a].at[:, columns(source, h)],
+            dst_ref=outs[a].at[source * heads + h],
             send_sem=out_send.at[a, h, peer],
             recv_sem=out_recv.at[a, h, source],
             device_id=(s, peer),
@@ -85,7 +85,7 @@
     def out_local(a, h):
         return pltpu.make_async_copy(
             stages[a].at[h, pl.ds(pl.multiple_of(z * rows, 32), rows), :],
-            outs[a].at[:, columns(z, h)],
+            outs[a].at[z * heads + h],
             out_loc.at[a, h],
         )
 
@@ -325,7 +325,8 @@
 
 def place_results(*refs):
     for a in range(4):
-        refs[4 + a][...] = refs[a][...]
+        for g in range(refs[a].shape[0]):
+            refs[4 + a][:, g * HD : (g + 1) * HD] = refs[a][g]
 
 
 def shards(nseq, nz, queries, keys, values, cotangent, neighbours):
@@ -335,7 +336,7 @@
     dma = pltpu.SemaphoreType.DMA
     results = pl.pallas_call(
         functools.partial(kernel, nseq, nz, heads, rows),
-        out_shape=[jax.ShapeDtypeStruct((rows, width), BF16)] * 4,
+        out_shape=[jax.ShapeDtypeStruct((width // HD, rows, HD), BF16)] * 4,
         in_specs=[place] * 4 + [pl.BlockSpec(memory_space=pltpu.VMEM)],
         out_specs=[place] * 4,
         scratch_shapes=[
@@ -371,11 +372,12 @@
     )(keys, values, queries, cotangent, neighbours.T)
     block_rows = 48 if rows % 48 == 0 else rows
     block = pl.BlockSpec((block_rows, width), lambda i: (i, 0))
+    by_head = pl.BlockSpec((width // HD, block_rows, HD), lambda i: (0, i, 0))
     return pl.pallas_call(
         place_results,
         grid=(rows // block_rows,),
         out_shape=[jax.ShapeDtypeStruct((rows, width), BF16)] * 4,
-        in_specs=[block] * 4,
+        in_specs=[by_head] * 4,
         out_specs=[block] * 4,
         compiler_params=pltpu.CompilerParams(vmem_limit_bytes=56 * 1024 * 1024),
     )(*results)

time: 150 us -> 150 us (level)
  no operation moved by 1% of the time
where the time goes in v6:
time: 150 us; the launch traced here: 149 us
  Pallas kernels  148 us (99%)
    pallas_call x1, Pallas kernels, shards(): pl.pallas_call(functools.partial(kernel, nseq, nz, heads, rows), out_shap...  144 us
    pallas_call x1, Pallas kernels, shards(): pl.pallas_call(place_results, grid=(rows // block_rows,), out_shape=[jax....  4.43 us

profile of v6, /device:TPU:2, one launch (start us, length us, event | category | flops | bytes accessed | tf_op | source)
XLA Modules:
  0.0 148.6 jit_solution(11130177840875753071)
XLA Ops:
  0.6 143.6 %shard_map.84 = (bf16[16,192,128]{2,1,0:T(8,128)(2,1)}, bf16[16,192,128]{2,1,0:T(8,128)(2,1)}, bf16[16,192,128]{2,1,0:T(8,128)(2,1)}, bf16[16,192,128]{2,1,0:T(8,128)(2,1)}) custom-call(bf16[192,2048]{1,0:T(8,128)(2,1)} %k_in.1, bf16[192,2048]{1,0:T(8,128)(2,1)} %v_in.1, bf16[192,2048]{1,0:T(8,128)(2,1)} %q_in.1, bf16[192,2048]{1,0:T(8,128)(2,1)} %c_in.1, ...), custom_call_target="tpu_custom_call" | custom-call | tf_op jit(solution)/shard_map/pallas_call | solution.py:337
  144.2 4.4 %shard_map.85 = (bf16[192,2048]{1,0:T(8,128)(2,1)}, bf16[192,2048]{1,0:T(8,128)(2,1)}, bf16[192,2048]{1,0:T(8,128)(2,1)}, bf16[192,2048]{1,0:T(8,128)(2,1)}) custom-call(bf16[16,192,128]{2,1,0:T(8,128)(2,1)} %get-tuple-element.8.refs_0_, bf16[16,192,128]{2,1,0:T(8,128)(2,1)} %get-tuple-element.9.refs_1_, bf16[16,192,128]{2,1,0:T(8,128)(2,1)} %get-tuple-element.10.refs_2_, ...), custom_call_target="tpu_custom_call" | custom-call | tf_op jit(solution)/shard_map/pallas_call | solution.py:376

commit v7 on v5

--- a/solution.py
+++ b/solution.py
@@ -43,7 +43,8 @@
     scale = 1.0 / math.sqrt(HD)
     log2_scale = scale * math.log2(math.e)
 
-    peers = [lax.rem(z + d, nz) for d in range(1, nz)]
+    far_first = sorted(range(1, nz), key=lambda d: abs(2 * d - nz))
+    peers = [lax.rem(z + d, nz) for d in far_first]
     ins = (k_in, v_in, q_in, c_in)
     outs = (o_out, gq_out, gk_out, gv_out)
     stages = (o_st, gq_st, gk_st, gv_st)

time: 150 us -> 150 us (level)
  no operation moved by 1% of the time
where the time goes in v7:
time: 150 us; the launch traced here: 149 us
  Pallas kernels  148 us (99%)
    pallas_call x1, Pallas kernels, shards(): pl.pallas_call(functools.partial(kernel, nseq, nz, heads, rows), out_shap...  144 us
    pallas_call x1, Pallas kernels, shards(): pl.pallas_call(place_results, grid=(rows // block_rows,), out_shape=[jax....  4.24 us

profile of v7, /device:TPU:2, one launch (start us, length us, event | category | flops | bytes accessed | tf_op | source)
XLA Modules:
  0.0 148.5 jit_solution(12830609621266275366)
XLA Ops:
  0.6 143.6 %shard_map.84 = (bf16[192,2048]{1,0:T(8,128)(2,1)}, bf16[192,2048]{1,0:T(8,128)(2,1)}, bf16[192,2048]{1,0:T(8,128)(2,1)}, bf16[192,2048]{1,0:T(8,128)(2,1)}) custom-call(bf16[192,2048]{1,0:T(8,128)(2,1)} %k_in.1, bf16[192,2048]{1,0:T(8,128)(2,1)} %v_in.1, bf16[192,2048]{1,0:T(8,128)(2,1)} %q_in.1, bf16[192,2048]{1,0:T(8,128)(2,1)} %c_in.1, s32[27,96]{1,0:T(8,128)} %bitcast.1), custom_call_target="tpu_custom_call" | custom-call | tf_op jit(solution)/shard_map/pallas_call | solution.py:337
  144.3 4.2 %shard_map.85 = (bf16[192,2048]{1,0:T(8,128)(2,1)}, bf16[192,2048]{1,0:T(8,128)(2,1)}, bf16[192,2048]{1,0:T(8,128)(2,1)}, bf16[192,2048]{1,0:T(8,128)(2,1)}) custom-call(bf16[192,2048]{1,0:T(8,128)(2,1)} %get-tuple-element.8.refs_0_, bf16[192,2048]{1,0:T(8,128)(2,1)} %get-tuple-element.9.refs_1_, bf16[192,2048]{1,0:T(8,128)(2,1)} %get-tuple-element.10.refs_2_, ...), custom_call_target="tpu_custom_call" | custom-call | tf_op jit(solution)/shard_map/pallas_call | solution.py:375
